TPU v7x, 128 devices: a whole 4x4x4 slice. The times are simulated.
128 devices in a mesh: dp: 8 (over z, core), mp: 16 (over y, x).
Axes of the slice: x: 4, y: 4, z: 4, core: 2. Of those that a mesh axis runs over, the one named last changes fastest.
Arguments:
- gradient: bfloat16 [80, 262144], P(None, ('dp', 'mp')), may hold values from -1500 to 1500
- owner_device: int32 [80], replicated, may hold values from 0 to 127, as said below
- state_slot: int32 [80], replicated, may hold values from 0 to 1
- left_stat: float32 [256, 512, 512], P(('dp', 'mp')), may hold values from -8 to 10, as said below
- right_stat: float32 [256, 512, 512], P(('dp', 'mp')), may hold values from -8 to 10, as said below
- left_basis: float32 [256, 512, 512], P(('dp', 'mp')), may hold values from -1 to 1, as said below
- right_basis: float32 [256, 512, 512], P(('dp', 'mp')), may hold values from -1 to 1, as said below
- moment: float32 [256, 512, 512], P(('dp', 'mp')), may hold values from -4 to 4
- second_moment: float32 [256, 512, 512], P(('dp', 'mp')), may hold values from 0.2 to 5
Outputs:
- new_left_stat: float32 [256, 512, 512], P(('dp', 'mp'))
- new_right_stat: float32 [256, 512, 512], P(('dp', 'mp'))
- new_left_basis: float32 [256, 512, 512], P(('dp', 'mp'))
- new_right_basis: float32 [256, 512, 512], P(('dp', 'mp'))
- new_moment: float32 [256, 512, 512], P(('dp', 'mp'))
- new_second_moment: float32 [256, 512, 512], P(('dp', 'mp'))
- direction: float32 [80, 262144], P(None, ('dp', 'mp'))
Inputs may be any that keep to these rules, and one draw needn't show every extreme that they name: Block b's state is slot state_slot[b] of device owner_device[b], devices counted in dp+mp order; no two blocks share a slot. Devices 2k and 2k + 1 hold at most 2 blocks together, the first two and the last two devices hold one block each, and some devices hold 2. `left_stat`: symmetric positive definite. `right_stat`: symmetric positive definite. `left_basis`: orthogonal matrices. `right_basis`: orthogonal matrices.
All inputs are finite; a program needn't handle non-finite values.
Results may differ from a plain program's by a relative error of at most 0.0003.
Values may be sent and summed in bfloat16 or wider, within the bound.
A program may use at most 128 MiB of HBM per device.

v0:
```python
import functools

import jax
import jax.numpy as jnp
from jax import lax
from jax.experimental import pallas as pl
from jax.experimental.pallas import tpu as pltpu
from jax.sharding import PartitionSpec as P

N = 512
D = 128
LB = 32
PIECE = 2048
F32 = jnp.float32
BF16 = jnp.bfloat16
KEEP = 0.9
MIX = 1.0 - KEEP
STABILITY = 1e-08


def split(x):
    hi = x.astype(BF16)
    lo = (x - hi.astype(F32)).astype(BF16)
    return hi, lo


def dot3(a, b, ca, cb):
    dims = (((ca,), (cb,)), ((), ()))
    d = lambda x, y: lax.dot_general(x, y, dims, preferred_element_type=F32)
    return d(a[0], b[0]) + (d(a[0], b[1]) + d(a[1], b[0]))


def finish(ws, s, lb):
    lanes = lax.broadcasted_iota(jnp.int32, (lb, D), 1)
    on = lanes == lax.broadcasted_iota(jnp.int32, (lb, D), 0) + s * lb
    out = []
    for d, e in ws:
        piv = jnp.sum(jnp.where(on, d, 0.0), axis=1, keepdims=True)
        r = lax.rsqrt(piv)
        out.append((d * r, e * r))
    return out


def leaf(ws, s, lb):
    n = len(ws)
    sub = lax.broadcasted_iota(jnp.int32, (8, D), 0)
    ng = lb // 8
    ws = [([d[8 * i:8 * i + 8] for i in range(ng)], [e[8 * i:8 * i + 8] for i in range(ng)]) for d, e in ws]
    for g in range(ng):
        bc = []
        for b in range(n):
            ds, es = ws[b]
            bc.append([[jnp.broadcast_to(ds[i][:, s * lb + 8 * g + j:s * lb + 8 * g + j + 1], (8, D)) for i in range(g, ng)] for j in range(8)])
        for k in range(8):
            for b in range(n):
                ds, es = ws[b]
                cols = bc[b]
                own = cols[k]
                rp = 1.0 / jnp.broadcast_to(own[0][k:k + 1, :], (8, D))
                m = [x * rp for x in own]
                m[0] = jnp.where(sub > k, m[0], 0.0)
                for j in range(k + 1, 8):
                    w = jnp.broadcast_to(own[0][j:j + 1, :], (8, D))
                    cols[j] = [x - y * w for x, y in zip(cols[j], m)]
                rd = jnp.broadcast_to(ds[g][k:k + 1, :], (8, D))
                re = jnp.broadcast_to(es[g][k:k + 1, :], (8, D))
                for i in range(g, ng):
                    if i == g and k == 7:
                        continue
                    ds[i] = ds[i] - m[i - g] * rd
                    es[i] = es[i] - m[i - g] * re
    ws = [(jnp.concatenate(ds, axis=0), jnp.concatenate(es, axis=0)) for ds, es in ws]
    return finish(ws, s, lb)


def dot2(a, b, ca, cb):
    dims = (((ca,), (cb,)), ((), ()))
    d = lambda x, y: lax.dot_general(x, y, dims, preferred_element_type=F32)
    return d(a, b[0]) + d(a, b[1])


def dot2l(a, b, ca, cb):
    dims = (((ca,), (cb,)), ((), ()))
    d = lambda x, y: lax.dot_general(x, y, dims, preferred_element_type=F32)
    return d(a[0], b) + d(a[1], b)


def travel_kernel(devices, mp, code, grad, ls_h, lb_h, rs_h, rb_h, m_h, v_h,
                  a_h, p_h, g_h, rot_h, step_h, clip_out,
                  stage, away, arr, sq, sqs, x_s, st, bs, mo, vs, g_s, ps, gram, rots, steps,
                  in_sem, out_sem, send_sem, recv_sem):
    me = lax.axis_index("dp") * mp + lax.axis_index("mp")
    place = lambda d: {"dp": lax.div(d, mp), "mp": lax.rem(d, mp)}
    barrier = pltpu.get_barrier_semaphore()

    def greet(i, carry):
        pl.semaphore_signal(barrier, inc=1, device_id=place(lax.rem(me + i, devices)), device_id_type=pl.DeviceIdType.MESH)
        return carry

    lax.fori_loop(1, devices, greet, 0)
    ins = [(lb_h, bs.at[pl.ds(0, 2)]), (ls_h, st.at[pl.ds(0, 2)]), (rb_h, bs.at[pl.ds(2, 2)]), (rs_h, st.at[pl.ds(2, 2)]), (m_h, mo), (v_h, vs)]
    loads = [pltpu.make_async_copy(src, dst, in_sem.at[n]) for n, (src, dst) in enumerate(ins)]
    for c in loads:
        c.start()

    g = grad[...]
    for s in range(2):
        names = lax.broadcasted_iota(jnp.int32, (devices, code.shape[1]), 0) + s * devices
        picker = (names == code[...]).astype(BF16)
        row = jnp.dot(picker, g, preferred_element_type=F32)
        for r in range(16):
            stage[s, pl.ds(r, devices, stride=16), :] = row[:, r * D:(r + 1) * D]
        away[s] = stage[s].astype(BF16).reshape(devices, 16, D)
    gf = g.astype(F32)
    own = jnp.sum(jnp.sum(gf * gf, axis=1, keepdims=True), axis=0, keepdims=True)
    sq[0] = jnp.broadcast_to(own, (1, D))
    sqs[me] = sq[0]
    pl.semaphore_wait(barrier, devices - 1)

    def send(src, dst, n):
        def one(i, carry):
            to = lax.rem(me + i, devices)
            pltpu.make_async_remote_copy(
                src_ref=src(to), dst_ref=dst, send_sem=send_sem.at[n], recv_sem=recv_sem.at[n],
                device_id=place(to), device_id_type=pl.DeviceIdType.MESH,
            ).start()
            return carry

        lax.fori_loop(1, devices, one, 0)

    send(lambda to: away.at[0, to], arr.at[0, me], 0)
    send(lambda to: sq.at[0], sqs.at[me], 2)
    send(lambda to: away.at[1, to], arr.at[1, me], 1)
    keep = [pltpu.make_async_copy(away.at[s, me], arr.at[s, me], in_sem.at[6 + s]) for s in range(2)]
    for c in keep:
        c.start()

    for c in loads[:4]:
        c.wait()
    for b in range(4):
        ps[b] = KEEP * dot3(split(st[b]), split(bs[b]), 1, 0)
    loads[4].wait()
    for s in range(2):
        rots[s] = dot3(split(dot3(split(bs[s]), split(mo[s]), 0, 0)), split(bs[2 + s]), 1, 0)
    loads[5].wait()
    most = pl.ds(0, devices - 1)
    outs = []

    def put(src, dst):
        outs.append(pltpu.make_async_copy(src, dst, out_sem.at[len(outs)]))
        outs[-1].start()

    for s in range(2):
        pltpu.make_async_copy(arr.at[s, most], arr.at[s, most], recv_sem.at[s]).wait()
        keep[s].wait()
        if s == 0:
            pltpu.make_async_copy(sqs.at[most], sqs.at[most], recv_sem.at[2]).wait()
            mean = jnp.sum(sqs[...], axis=0) / (80.0 * N * N)
            clips = 1.0 / jnp.maximum(1.0, jnp.sqrt(mean))
            clip_out[...] = jnp.broadcast_to(clips, (8, D))
            clip = clips[:, 0:1]
            weight = (MIX / N) * clip * clip
        stage[s] = arr[s].astype(F32).reshape(16 * devices, D)
        for q in range(4):
            for c in range(4):
                x_s[c, pl.ds(q, D, stride=4), :] = stage[s, pl.ds(4 * q + c, devices, stride=16), :]
        for c in range(4):
            g_s[s, :, c * D:(c + 1) * D] = x_s[c].astype(BF16)
        put(g_s.at[s], g_h.at[s])
        g = g_s[s]
        l, r = split(bs[s]), split(bs[2 + s])
        t = split(dot2l(l, g, 0, 0))
        rot = clip * dot3(t, r, 1, 0)
        v = KEEP * vs[s] + MIX * rot * rot
        ratio = (KEEP * rots[s] + MIX * rot) / (jnp.sqrt(v) + STABILITY)
        rots[s] = rot
        put(rots.at[s], rot_h.at[s])
        step = dot3(split(dot3(l, split(ratio), 1, 0)), r, 1, 1)
        for c in range(4):
            x_s[c] = step[:, c * D:(c + 1) * D]
        for q in range(4):
            for c in range(4):
                steps[pl.ds(16 * s + 4 * q + c, devices, stride=32), :] = x_s[c, pl.ds(q, D, stride=4), :]
        p = ps[s] + weight * dot2(g, t, 1, 1)
        ps[s] = p
        put(ps.at[s], p_h.at[s])
        p = split(p)
        gram[s] = dot3(p, p, 0, 0)
        put(gram.at[s], a_h.at[s])
        p = ps[2 + s] + weight * dot2(g, split(dot2(g, r, 1, 0)), 0, 0)
        ps[2 + s] = p
        put(ps.at[2 + s], p_h.at[2 + s])
        p = split(p)
        gram[2 + s] = dot3(p, p, 0, 0)
        put(gram.at[2 + s], a_h.at[2 + s])
    put(steps, step_h)
    for s in range(2):
        pltpu.make_async_copy(arr.at[s, most], arr.at[s, most], send_sem.at[s]).wait()
    pltpu.make_async_copy(sqs.at[most], sqs.at[most], send_sem.at[2]).wait()
    for c in outs:
        c.wait()


def travel(code, gradient, left_stat, left_basis, right_stat, right_basis, moment, second):
    devices, mp = lax.axis_size(("dp", "mp")), lax.axis_size("mp")
    vm = pl.BlockSpec(memory_space=pltpu.VMEM)
    hb = pl.BlockSpec(memory_space=pl.ANY)
    four = jax.ShapeDtypeStruct((4, N, N), F32)
    two = jax.ShapeDtypeStruct((2, N, N), F32)
    return pl.pallas_call(
        functools.partial(travel_kernel, devices, mp),
        out_shape=[
            four, four, jax.ShapeDtypeStruct((2, N, N), BF16), two,
            jax.ShapeDtypeStruct((32 * devices, D), F32), jax.ShapeDtypeStruct((8, D), F32),
        ],
        in_specs=[vm, vm] + [hb] * 6,
        out_specs=[hb] * 5 + [vm],
        scratch_shapes=[
            pltpu.VMEM((2, 16 * devices, D), F32),
            pltpu.VMEM((2, devices, 16, D), BF16),
            pltpu.VMEM((2, devices, 16, D), BF16),
            pltpu.VMEM((1, 1, D), F32),
            pltpu.VMEM((devices, 1, D), F32),
            pltpu.VMEM((4, N, D), F32),
            pltpu.VMEM((4, N, N), F32),
            pltpu.VMEM((4, N, N), F32),
            pltpu.VMEM((2, N, N), F32),
            pltpu.VMEM((2, N, N), F32),
            pltpu.VMEM((2, N, N), BF16),
            pltpu.VMEM((4, N, N), F32),
            pltpu.VMEM((4, N, N), F32),
            pltpu.VMEM((2, N, N), F32),
            pltpu.VMEM((32 * devices, D), F32),
            pltpu.SemaphoreType.DMA((8,)),
            pltpu.SemaphoreType.DMA((13,)),
            pltpu.SemaphoreType.DMA((3,)),
            pltpu.SemaphoreType.DMA((3,)),
        ],
        compiler_params=pltpu.CompilerParams(
            vmem_limit_bytes=56 << 20, collective_id=0, has_side_effects=True
        ),
        cost_estimate=pl.CostEstimate(flops=70 * 2 * N**3, bytes_accessed=32 * N * N * 4, transcendentals=0),
        name="travel",
    )(code, gradient, left_stat, left_basis, right_stat, right_basis, moment, second)


def refresh_kernel(live, clip_ref, g_ref, a_h, p_h, rot_h, ls_h, rs_h, lb_h, rb_h, m_h, v_h,
                   nls_h, nrs_h, nlb_h, nrb_h, nm_h, nv_h,
                   a_ref, p_ref, q_ref, w_d, w_e, st, bs, mo, vs, rots, in_sem, out_sem, q_sem):
    two = lambda ref, n: ref.at[pl.ds(n, 2)]
    ins = [(a_h, a_ref), (p_h, p_ref), (lb_h, two(bs, 0)), (rb_h, two(bs, 2)), (ls_h, two(st, 0)), (rs_h, two(st, 2)),
           (m_h, mo), (v_h, vs), (rot_h, rots)]
    loads = [pltpu.make_async_copy(src, dst, in_sem.at[i]) for i, (src, dst) in enumerate(ins)]
    for c in loads:
        c.start()
    clip = clip_ref[0:1, 0:1]
    weight = (MIX / N) * clip * clip
    gram = lambda g, c: lax.dot_general(g, g, (((c,), (c,)), ((), ())), preferred_element_type=F32)
    stores = [pltpu.make_async_copy(src, dst, out_sem.at[i]) for i, (src, dst) in enumerate(
        [(two(st, 0), nls_h), (two(st, 2), nrs_h), (mo, nm_h), (vs, nv_h)])]
    eye = (lax.broadcasted_iota(jnp.int32, (D, D), 0) == lax.broadcasted_iota(jnp.int32, (D, D), 1)).astype(F32)
    columns = lambda b, o: pltpu.make_async_copy(
        q_ref.at[b, :, pl.ds(o, D)], (nlb_h if b < 2 else nrb_h).at[b % 2, :, pl.ds(o, D)], q_sem.at[b, o // D])
    loads[0].wait()

    def step(k, carry):
        at = pl.ds(pl.multiple_of(k * D, D), D)
        for b in range(4):
            w_d[b] = a_ref[b, at, at]
            w_e[b] = eye
        for s in range(D // LB):
            here = slice(s * LB, (s + 1) * LB)
            ws = leaf([(w_d[b, here, :], w_e[b, here, :]) for b in range(4)], s, LB)
            for b in range(4):
                rd, re = ws[b]
                w_e[b, here, :] = re
                if s < D // LB - 1:
                    low = slice((s + 1) * LB, D)
                    dh, dl = split(rd)
                    eh, el = split(re)
                    lhs = jnp.concatenate([dh, dh, dl], axis=0)
                    rhs_d = jnp.concatenate([dh, dl, dh], axis=0)
                    rhs_e = jnp.concatenate([eh, el, eh], axis=0)
                    dims = (((0,), (0,)), ((), ()))
                    ud = lax.dot_general(lhs, rhs_d, dims, preferred_element_type=F32)
                    ue = lax.dot_general(lhs, rhs_e, dims, preferred_element_type=F32)
                    w_d[b, low, :] = w_d[b, low, :] - ud[(s + 1) * LB:, :]
                    w_e[b, low, :] = w_e[b, low, :] - ue[(s + 1) * LB:, :]
        for kk in range(N // D):
            @pl.when(k == kk)
            def _():
                o = kk * D
                if kk == 0:
                    for c in loads[1:4]:
                        c.wait()
                for b in range(4):
                    x = split(w_e[b])
                    q = dot3(split(p_ref[b, :, o:o + D]), x, 1, 1)
                    q_ref[b, :, o:o + D] = jnp.where(live[b % 2] > 0, q, bs[b, :, o:o + D])
                    columns(b, o).start()
                    if kk < N // D - 1:
                        r = split(dot3(x, split(a_ref[b, o:o + D, o + D:]), 1, 0))
                        for i in range(o + D, N, D):
                            rows = [y[:, i - o - D:i - o] for y in r]
                            rest = [y[:, i - o - D:] for y in r]
                            a_ref[b, i:i + D, i:] = a_ref[b, i:i + D, i:] - dot3(rows, rest, 0, 0)
                        p_ref[b, :, o + D:] = p_ref[b, :, o + D:] - dot3(split(q), r, 1, 0)
                if kk < 2:
                    loads[4 + kk].wait()
                    for s in range(2):
                        old = st[2 * kk + s]
                        st[2 * kk + s] = jnp.where(live[s] > 0, KEEP * old + weight * gram(g_ref[s], 1 - kk), old)
                    stores[kk].start()
                if kk == 2:
                    for c in loads[6:]:
                        c.wait()
                    for s in range(2):
                        mo[s] = jnp.where(live[s] > 0, KEEP * mo[s] + (MIX * clip) * g_ref[s].astype(F32), mo[s])
                        vs[s] = jnp.where(live[s] > 0, KEEP * vs[s] + MIX * rots[s] * rots[s], vs[s])
                    stores[2].start()
                    stores[3].start()
        return carry

    lax.fori_loop(0, N // D, step, 0)
    for c in stores:
        c.wait()
    for b in range(4):
        for o in range(0, N, D):
            columns(b, o).wait()


def refresh(live, clip, g, a, p, rot, left_stat, right_stat, left_basis, right_basis, moment, second):
    vm = pl.BlockSpec(memory_space=pltpu.VMEM)
    hb = pl.BlockSpec(memory_space=pl.ANY)
    return pl.pallas_call(
        refresh_kernel,
        out_shape=[jax.ShapeDtypeStruct((2, N, N), F32)] * 6,
        in_specs=[pl.BlockSpec(memory_space=pltpu.SMEM)] + [vm] * 2 + [hb] * 9,
        out_specs=[hb] * 6,
        scratch_shapes=[
            pltpu.VMEM((4, N, N), F32),
            pltpu.VMEM((4, N, N), F32),
            pltpu.VMEM((4, N, N), F32),
            pltpu.VMEM((4, D, D), F32),
            pltpu.VMEM((4, D, D), F32),
            pltpu.VMEM((4, N, N), F32),
            pltpu.VMEM((4, N, N), F32),
            pltpu.VMEM((2, N, N), F32),
            pltpu.VMEM((2, N, N), F32),
            pltpu.VMEM((2, N, N), F32),
            pltpu.SemaphoreType.DMA((9,)),
            pltpu.SemaphoreType.DMA((4,)),
            pltpu.SemaphoreType.DMA((4, N // D)),
        ],
        compiler_params=pltpu.CompilerParams(vmem_limit_bytes=56 << 20),
        cost_estimate=pl.CostEstimate(flops=100 * 2 * N**3, bytes_accessed=30 * N * N * 4, transcendentals=0),
        name="refresh",
    )(live, clip, g, a, p, rot, left_stat, right_stat, left_basis, right_basis, moment, second)


def shards(
    gradient,
    owner_device,
    state_slot,
    left_stat,
    right_stat,
    left_basis,
    right_basis,
    moment,
    second_moment,
):
    devices = lax.axis_size(("dp", "mp"))
    slot_count = left_stat.shape[0]
    flat_piece = gradient.shape[1]
    my_index = lax.axis_index(("dp", "mp"))
    slot_code = state_slot * devices + owner_device
    live = jnp.any(
        (owner_device[None, :] == my_index)
        & (state_slot[None, :] == jnp.arange(slot_count, dtype=jnp.int32)[:, None]),
        axis=1,
    ).astype(jnp.int32)
    a, p, g, rot, steps, clip = travel(
        slot_code[None, :], gradient, left_stat, left_basis, right_stat, right_basis, moment, second_moment
    )
    steps = steps.reshape(devices, 32, D)
    backward = lax.all_to_all(steps, ("dp", "mp"), split_axis=0, concat_axis=0, tiled=True)
    new_left, new_right, new_left_basis, new_right_basis, new_moment, new_second = refresh(
        live, clip, g, a, p, rot, left_stat, right_stat, left_basis, right_basis, moment, second_moment
    )
    rows = backward.reshape(devices * slot_count, 16, D)
    direction = jnp.take(rows, owner_device * slot_count + state_slot, axis=0).reshape(-1, flat_piece)
    return (
        new_left,
        new_right,
        new_left_basis,
        new_right_basis,
        new_moment,
        new_second,
        direction,
    )


def solution(mesh):
    spread = P(("dp", "mp"), None, None)
    flat = P(None, ("dp", "mp"))
    return jax.shard_map(
        shards,
        mesh=mesh,
        in_specs=(flat, P(), P()) + (spread,) * 6,
        out_specs=(spread,) * 6 + (flat,),
        check_vma=False,
    )
```

profile of v0, /device:TPU:1, one launch (start us, length us, event | category | flops | bytes accessed | tf_op | source)
XLA Modules:
  0.0 93.3 jit_solution(8885093754837528506)
XLA Ops:
  0.6 1.2 %add_bitcast_fusion.code = s32[1,80]{1,0:T(1,128)} fusion(s32[80]{0:T(128)} %param.10, s32[80]{0:T(128)} %param.11), kind=kLoop, calls=%fused_computation.6 | loop fusion | flops 160 | bytes 960 | tf_op jit(solution)/shard_map/broadcast_in_dim | solution.py:383
  1.8 46.4 %travel.1 = (f32[4,512,512]{2,1,0:T(8,128)}, f32[4,512,512]{2,1,0:T(8,128)}, bf16[2,512,512]{2,1,0:T(8,128)(2,1)}, f32[2,512,512]{2,1,0:T(8,128)}, f32[4096,128]{1,0:T(8,128)}, /*index=5*/f32[8,128]{1,0:T(8,128)}) custom-call(s32[1,80]{1,0:T(1,128)} %add_bitcast_fusion.code, bf16[80,2048]{1,0:T(8,128)(2,1)} %grad.1, f32[2,512,512]{2,1,0:T(8,128)} %ls_h.3, ...), custom_call_target="tpu_custom_call" | custom-call | flops 18790481920 | bytes 33554432 | tf_op jit(solution)/shard_map/travel/pallas_call | solution.py:210
  48.3 0.0 copy-start
  48.3 0.0 copy-start.1
  48.3 3.6 %all-to-all-start = ((f32[128,32,128]{2,1,0:T(8,128)}), f32[128,32,128]{2,1,0:T(8,128)S(1)}, u32[]{:S(2)}, u32[]{:S(2)}) async-start(f32[128,32,128]{2,1,0:T(8,128)} %bitcast.9), calls=%async_computation | async-start | bytes 4194304 | tf_op jit(solution)/shard_map/all_to_all | solution.py:386
  51.9 0.0 copy-done
  51.9 0.0 copy-done.1
  51.9 0.1 and_reduce_fusion
  52.0 0.5 convert_element_type.3.live
  52.6 39.0 %refresh.1 = (f32[2,512,512]{2,1,0:T(8,128)}, f32[2,512,512]{2,1,0:T(8,128)}, f32[2,512,512]{2,1,0:T(8,128)}, f32[2,512,512]{2,1,0:T(8,128)}, f32[2,512,512]{2,1,0:T(8,128)}, /*index=5*/f32[2,512,512]{2,1,0:T(8,128)}) custom-call(s32[2]{0:T(128)} %convert_element_type.3.live, f32[8,128]{1,0:T(8,128)} %get-tuple-element.19.clip_ref, ...), custom_call_target="tpu_custom_call" | custom-call | flops 26843545600 | bytes 31457280 | tf_op jit(solution)/shard_map/refresh/pallas_call | solution.py:335
  91.5 0.0 all-to-all-done
  91.5 0.7 gather_fusion
  92.2 1.1 %bitcast_select_fusion = f32[80,2048]{1,0:T(8,128)} fusion(f32[10,8,16,128]{3,2,1,0:T(8,128)S(1)} %bitcast.8, pred[80]{0:T(512)(128)(4,1)S(1)} %get-tuple-element.31), kind=kLoop, calls=%fused_computation.1 | loop fusion | flops 163840 | bytes 1310800 | tf_op jit(solution)/shard_map/jit(_take)/select_n | solution.py:391
  (2 shorter events, 0.0 us)
Async XLA Ops:
  48.3 3.6 %copy-start = (s32[80]{0:T(128)S(1)}, s32[80]{0:T(128)}, u32[]{:S(2)}) copy-start(s32[80]{0:T(128)} %param.10) | copy-start | bytes 964
  48.3 3.6 %copy-start.1 = (s32[80]{0:T(128)S(1)}, s32[80]{0:T(128)}, u32[]{:S(2)}) copy-start(s32[80]{0:T(128)} %param.11) | copy-start | bytes 964
  48.3 43.3 %all-to-all-start = ((f32[128,32,128]{2,1,0:T(8,128)}), f32[128,32,128]{2,1,0:T(8,128)S(1)}, u32[]{:S(2)}, u32[]{:S(2)}) async-start(f32[128,32,128]{2,1,0:T(8,128)} %bitcast.9), calls=%async_computation | async-start | bytes 4194304 | tf_op jit(solution)/shard_map/all_to_all | solution.py:386
where the time goes:
time: 93.6 us; the launch traced here: 93.3 us
  Pallas kernels  85.4 us (91%)
  starting transfers between devices  3.59 us (4%)
  other arithmetic  2.92 us (3%)
    pallas_call x1, Pallas kernels, travel(): pl.pallas_call(functools.partial(travel_kernel, devices, mp), out_shape=[...  46.4 us
    pallas_call x1, Pallas kernels, refresh(): pl.pallas_call(refresh_kernel, out_shape=[jax.ShapeDtypeStruct((2, N, N),...  39 us
    all_to_all x1, starting transfers between devices, shards(): lax.all_to_all(steps, ('dp', 'mp'), split_axis=0, concat_axis=0, tiled=True)  3.59 us
  transfers between devices with their start and end apart: 1, of which 0 were waited for; matrix products, arithmetic and copies ran while one was open for 1% of the time, Pallas kernels for 42%

commit v1 on v0

--- a/solution.py
+++ b/solution.py
@@ -9,7 +9,7 @@
 
 N = 512
 D = 128
-LB = 32
+LB = 16
 PIECE = 2048
 F32 = jnp.float32
 BF16 = jnp.bfloat16
@@ -26,51 +26,47 @@
 
 def dot3(a, b, ca, cb):
     dims = (((ca,), (cb,)), ((), ()))
-    d = lambda x, y: lax.dot_general(x, y, dims, preferred_element_type=F32)
-    return d(a[0], b[0]) + (d(a[0], b[1]) + d(a[1], b[0]))
-
-
-def finish(ws, s, lb):
-    lanes = lax.broadcasted_iota(jnp.int32, (lb, D), 1)
-    on = lanes == lax.broadcasted_iota(jnp.int32, (lb, D), 0) + s * lb
-    out = []
-    for d, e in ws:
-        piv = jnp.sum(jnp.where(on, d, 0.0), axis=1, keepdims=True)
-        r = lax.rsqrt(piv)
-        out.append((d * r, e * r))
-    return out
+    return lax.dot_general(jnp.concatenate([a[0], a[0], a[1]], axis=ca), jnp.concatenate([b[0], b[1], b[0]], axis=cb), dims, preferred_element_type=F32)
 
 
 def leaf(ws, s, lb):
     n = len(ws)
     sub = lax.broadcasted_iota(jnp.int32, (8, D), 0)
+    lane = lax.broadcasted_iota(jnp.int32, (8, D), 1)
     ng = lb // 8
-    ws = [([d[8 * i:8 * i + 8] for i in range(ng)], [e[8 * i:8 * i + 8] for i in range(ng)]) for d, e in ws]
+    ws = [[w[8 * i:8 * i + 8] for i in range(ng)] for w in ws]
+    pv = [[None] * ng for _ in range(n)]
     for g in range(ng):
-        bc = []
-        for b in range(n):
-            ds, es = ws[b]
-            bc.append([[jnp.broadcast_to(ds[i][:, s * lb + 8 * g + j:s * lb + 8 * g + j + 1], (8, D)) for i in range(g, ng)] for j in range(8)])
+        c0 = s * lb + 8 * g
+        bc = [[[jnp.broadcast_to(w[i][:, c0 + j:c0 + j + 1], (8, D)) for i in range(g, ng)] for j in range(8)] for w in ws]
         for k in range(8):
             for b in range(n):
-                ds, es = ws[b]
+                w = ws[b]
                 cols = bc[b]
                 own = cols[k]
-                rp = 1.0 / jnp.broadcast_to(own[0][k:k + 1, :], (8, D))
+                p = jnp.broadcast_to(own[0][k:k + 1, :], (8, D))
+                rp = 1.0 / p
+                pv[b][g] = p if k == 0 else jnp.where(sub >= k, p, pv[b][g])
                 m = [x * rp for x in own]
                 m[0] = jnp.where(sub > k, m[0], 0.0)
                 for j in range(k + 1, 8):
-                    w = jnp.broadcast_to(own[0][j:j + 1, :], (8, D))
-                    cols[j] = [x - y * w for x, y in zip(cols[j], m)]
-                rd = jnp.broadcast_to(ds[g][k:k + 1, :], (8, D))
-                re = jnp.broadcast_to(es[g][k:k + 1, :], (8, D))
+                    f = jnp.broadcast_to(own[0][j:j + 1, :], (8, D))
+                    cols[j] = [x - y * f for x, y in zip(cols[j], m)]
+                row = jnp.where(lane == c0 + k, 1.0, jnp.broadcast_to(w[g][k:k + 1, :], (8, D)))
                 for i in range(g, ng):
                     if i == g and k == 7:
                         continue
-                    ds[i] = ds[i] - m[i - g] * rd
-                    es[i] = es[i] - m[i - g] * re
-    ws = [(jnp.concatenate(ds, axis=0), jnp.concatenate(es, axis=0)) for ds, es in ws]
-    return finish(ws, s, lb)
+                    w[i] = jnp.where(lane == c0 + k, 0.0, w[i]) - m[i - g] * row
+    out = []
+    for b in range(n):
+        rows = []
+        for g in range(ng):
+            diag = sub + (s * lb + 8 * g)
+            w = ws[b][g]
+            w = jnp.where(lane == diag, 1.0, jnp.where((lane > diag) & (lane < (s + 1) * lb), 0.0, w))
+            rows.append(w * lax.rsqrt(pv[b][g]))
+        out.append(jnp.concatenate(rows, axis=0))
+    return out
 
 
 def dot2(a, b, ca, cb):
@@ -85,7 +81,7 @@
     return d(a[0], b) + d(a[1], b)
 
 
-def travel_kernel(devices, mp, code, grad, ls_h, lb_h, rs_h, rb_h, m_h, v_h,
+def travel_kernel(devices, mp, owner, slot, grad, ls_h, lb_h, rs_h, rb_h, m_h, v_h,
                   a_h, p_h, g_h, rot_h, step_h, clip_out,
                   stage, away, arr, sq, sqs, x_s, st, bs, mo, vs, g_s, ps, gram, rots, steps,
                   in_sem, out_sem, send_sem, recv_sem):
@@ -105,8 +101,8 @@
 
     g = grad[...]
     for s in range(2):
-        names = lax.broadcasted_iota(jnp.int32, (devices, code.shape[1]), 0) + s * devices
-        picker = (names == code[...]).astype(BF16)
+        names = lax.broadcasted_iota(jnp.int32, (devices, owner.shape[1]), 0)
+        picker = ((names == owner[...]) & (slot[...] == s)).astype(BF16)
         row = jnp.dot(picker, g, preferred_element_type=F32)
         for r in range(16):
             stage[s, pl.ds(r, devices, stride=16), :] = row[:, r * D:(r + 1) * D]
@@ -149,6 +145,14 @@
     def put(src, dst):
         outs.append(pltpu.make_async_copy(src, dst, out_sem.at[len(outs)]))
         outs[-1].start()
+
+    half = N // 2
+
+    def upper(b, p):
+        gram[b, :half] = dot3([y[:, :half] for y in p], p, 0, 0)
+        gram[b, half:, :half] = jnp.zeros((half, half), F32)
+        low = [y[:, half:] for y in p]
+        gram[b, half:, half:] = dot3(low, low, 0, 0)
 
     for s in range(2):
         pltpu.make_async_copy(arr.at[s, most], arr.at[s, most], recv_sem.at[s]).wait()
@@ -185,13 +189,13 @@
         ps[s] = p
         put(ps.at[s], p_h.at[s])
         p = split(p)
-        gram[s] = dot3(p, p, 0, 0)
+        upper(s, p)
         put(gram.at[s], a_h.at[s])
         p = ps[2 + s] + weight * dot2(g, split(dot2(g, r, 1, 0)), 0, 0)
         ps[2 + s] = p
         put(ps.at[2 + s], p_h.at[2 + s])
         p = split(p)
-        gram[2 + s] = dot3(p, p, 0, 0)
+        upper(2 + s, p)
         put(gram.at[2 + s], a_h.at[2 + s])
     put(steps, step_h)
     for s in range(2):
@@ -201,7 +205,7 @@
         c.wait()
 
 
-def travel(code, gradient, left_stat, left_basis, right_stat, right_basis, moment, second):
+def travel(owner, slot, gradient, left_stat, left_basis, right_stat, right_basis, moment, second):
     devices, mp = lax.axis_size(("dp", "mp")), lax.axis_size("mp")
     vm = pl.BlockSpec(memory_space=pltpu.VMEM)
     hb = pl.BlockSpec(memory_space=pl.ANY)
@@ -213,7 +217,7 @@
             four, four, jax.ShapeDtypeStruct((2, N, N), BF16), two,
             jax.ShapeDtypeStruct((32 * devices, D), F32), jax.ShapeDtypeStruct((8, D), F32),
         ],
-        in_specs=[vm, vm] + [hb] * 6,
+        in_specs=[vm] * 3 + [hb] * 6,
         out_specs=[hb] * 5 + [vm],
         scratch_shapes=[
             pltpu.VMEM((2, 16 * devices, D), F32),
@@ -241,12 +245,12 @@
         ),
         cost_estimate=pl.CostEstimate(flops=70 * 2 * N**3, bytes_accessed=32 * N * N * 4, transcendentals=0),
         name="travel",
-    )(code, gradient, left_stat, left_basis, right_stat, right_basis, moment, second)
+    )(owner, slot, gradient, left_stat, left_basis, right_stat, right_basis, moment, second)
 
 
 def refresh_kernel(live, clip_ref, g_ref, a_h, p_h, rot_h, ls_h, rs_h, lb_h, rb_h, m_h, v_h,
                    nls_h, nrs_h, nlb_h, nrb_h, nm_h, nv_h,
-                   a_ref, p_ref, q_ref, w_d, w_e, st, bs, mo, vs, rots, in_sem, out_sem, q_sem):
+                   a_ref, p_ref, q_ref, w_d, qs, rs, st, bs, mo, vs, rots, in_sem, out_sem, q_sem):
     two = lambda ref, n: ref.at[pl.ds(n, 2)]
     ins = [(a_h, a_ref), (p_h, p_ref), (lb_h, two(bs, 0)), (rb_h, two(bs, 2)), (ls_h, two(st, 0)), (rs_h, two(st, 2)),
            (m_h, mo), (v_h, vs), (rot_h, rots)]
@@ -258,43 +262,42 @@
     gram = lambda g, c: lax.dot_general(g, g, (((c,), (c,)), ((), ())), preferred_element_type=F32)
     stores = [pltpu.make_async_copy(src, dst, out_sem.at[i]) for i, (src, dst) in enumerate(
         [(two(st, 0), nls_h), (two(st, 2), nrs_h), (mo, nm_h), (vs, nv_h)])]
-    eye = (lax.broadcasted_iota(jnp.int32, (D, D), 0) == lax.broadcasted_iota(jnp.int32, (D, D), 1)).astype(F32)
+    lane = lax.broadcasted_iota(jnp.int32, (1, D), 1)
+    parts = D // LB
     columns = lambda b, o: pltpu.make_async_copy(
         q_ref.at[b, :, pl.ds(o, D)], (nlb_h if b < 2 else nrb_h).at[b % 2, :, pl.ds(o, D)], q_sem.at[b, o // D])
+    qs[...] = jnp.zeros_like(qs)
+    rs[...] = jnp.zeros_like(rs)
     loads[0].wait()
+    loads[1].wait()
 
     def step(k, carry):
         at = pl.ds(pl.multiple_of(k * D, D), D)
         for b in range(4):
             w_d[b] = a_ref[b, at, at]
-            w_e[b] = eye
-        for s in range(D // LB):
+        for s in range(parts):
             here = slice(s * LB, (s + 1) * LB)
-            ws = leaf([(w_d[b, here, :], w_e[b, here, :]) for b in range(4)], s, LB)
+            low = slice((s + 1) * LB, D)
+            ws = leaf([w_d[b, here, :] for b in range(4)], s, LB)
             for b in range(4):
-                rd, re = ws[b]
-                w_e[b, here, :] = re
-                if s < D // LB - 1:
-                    low = slice((s + 1) * LB, D)
-                    dh, dl = split(rd)
-                    eh, el = split(re)
-                    lhs = jnp.concatenate([dh, dh, dl], axis=0)
-                    rhs_d = jnp.concatenate([dh, dl, dh], axis=0)
-                    rhs_e = jnp.concatenate([eh, el, eh], axis=0)
-                    dims = (((0,), (0,)), ((), ()))
-                    ud = lax.dot_general(lhs, rhs_d, dims, preferred_element_type=F32)
-                    ue = lax.dot_general(lhs, rhs_e, dims, preferred_element_type=F32)
-                    w_d[b, low, :] = w_d[b, low, :] - ud[(s + 1) * LB:, :]
-                    w_e[b, low, :] = w_e[b, low, :] - ue[(s + 1) * LB:, :]
+                if b * parts // 4 == s:
+                    p_ref[b] = p_ref[b] - dot3((qs[0, b], qs[1, b]), (rs[0, b], rs[1, b]), 1, 0)
+            for b in range(4):
+                w_d[b, here, :] = jnp.where(lane < (s + 1) * LB, ws[b], 0.0)
+                if s < parts - 1:
+                    hi, lo = split(ws[b])
+                    u = dot3((hi, lo), (hi, lo), 0, 0)
+                    old = jnp.where((lane >= s * LB) & (lane < (s + 1) * LB), 0.0, w_d[b, low, :])
+                    w_d[b, low, :] = old - u[(s + 1) * LB:, :]
         for kk in range(N // D):
             @pl.when(k == kk)
             def _():
                 o = kk * D
                 if kk == 0:
-                    for c in loads[1:4]:
+                    for c in loads[2:4]:
                         c.wait()
                 for b in range(4):
-                    x = split(w_e[b])
+                    x = split(w_d[b])
                     q = dot3(split(p_ref[b, :, o:o + D]), x, 1, 1)
                     q_ref[b, :, o:o + D] = jnp.where(live[b % 2] > 0, q, bs[b, :, o:o + D])
                     columns(b, o).start()
@@ -304,7 +307,10 @@
                             rows = [y[:, i - o - D:i - o] for y in r]
                             rest = [y[:, i - o - D:] for y in r]
                             a_ref[b, i:i + D, i:] = a_ref[b, i:i + D, i:] - dot3(rows, rest, 0, 0)
-                        p_ref[b, :, o + D:] = p_ref[b, :, o + D:] - dot3(split(q), r, 1, 0)
+                        rs[0, b, :, o:o + D] = jnp.zeros((D, D), BF16)
+                        rs[1, b, :, o:o + D] = jnp.zeros((D, D), BF16)
+                        rs[0, b, :, o + D:], rs[1, b, :, o + D:] = r
+                        qs[0, b], qs[1, b] = split(q)
                 if kk < 2:
                     loads[4 + kk].wait()
                     for s in range(2):
@@ -342,7 +348,8 @@
             pltpu.VMEM((4, N, N), F32),
             pltpu.VMEM((4, N, N), F32),
             pltpu.VMEM((4, D, D), F32),
-            pltpu.VMEM((4, D, D), F32),
+            pltpu.VMEM((2, 4, N, D), BF16),
+            pltpu.VMEM((2, 4, D, N), BF16),
             pltpu.VMEM((4, N, N), F32),
             pltpu.VMEM((4, N, N), F32),
             pltpu.VMEM((2, N, N), F32),
@@ -373,14 +380,13 @@
     slot_count = left_stat.shape[0]
     flat_piece = gradient.shape[1]
     my_index = lax.axis_index(("dp", "mp"))
-    slot_code = state_slot * devices + owner_device
     live = jnp.any(
         (owner_device[None, :] == my_index)
         & (state_slot[None, :] == jnp.arange(slot_count, dtype=jnp.int32)[:, None]),
         axis=1,
     ).astype(jnp.int32)
     a, p, g, rot, steps, clip = travel(
-        slot_code[None, :], gradient, left_stat, left_basis, right_stat, right_basis, moment, second_moment
+        owner_device[None, :], state_slot[None, :], gradient, left_stat, left_basis, right_stat, right_basis, moment, second_moment
     )
     steps = steps.reshape(devices, 32, D)
     backward = lax.all_to_all(steps, ("dp", "mp"), split_axis=0, concat_axis=0, tiled=True)

time: 93.6 us -> 89.7 us (0.958)
  Pallas kernels: 85.4 us -> 82.7 us
  other arithmetic: 2.92 us -> 1.74 us
    pallas_call x1, Pallas kernels: 39 us -> 36.1 us  [refresh(): pl.pallas_call(refresh_kernel, out_shape=[jax.ShapeDtypeStruct((2, N, N),...]
    broadcast_in_dim x1 -> x0, other arithmetic: 1.19 us -> none  [shards(): slot_code[None, :]]
  transfers between devices with their start and end apart: 1 -> 1, of which waited for: 0 -> 0; matrix products, arithmetic and copies ran while one was open for 1% -> 1% of each run, Pallas kernels for 42% -> 40%
where the time goes in v1:
time: 89.7 us; the launch traced here: 89.4 us
  Pallas kernels  82.7 us (92%)
  starting transfers between devices  3.59 us (4%)
  other arithmetic  1.74 us (2%)
    pallas_call x1, Pallas kernels, travel(): pl.pallas_call(functools.partial(travel_kernel, devices, mp), out_shape=[...  46.6 us
    pallas_call x1, Pallas kernels, refresh(): pl.pallas_call(refresh_kernel, out_shape=[jax.ShapeDtypeStruct((2, N, N),...  36.1 us
    all_to_all x1, starting transfers between devices, shards(): lax.all_to_all(steps, ('dp', 'mp'), split_axis=0, concat_axis=0, tiled=True)  3.59 us
  transfers between devices with their start and end apart: 1, of which 0 were waited for; matrix products, arithmetic and copies ran while one was open for 1% of the time, Pallas kernels for 40%

profile of v1, /device:TPU:1, one launch (start us, length us, event | category | flops | bytes accessed | tf_op | source)
XLA Modules:
  0.0 89.4 jit_solution(17291215856503242393)
XLA Ops:
  0.6 46.6 %travel.1 = (f32[4,512,512]{2,1,0:T(8,128)}, f32[4,512,512]{2,1,0:T(8,128)}, bf16[2,512,512]{2,1,0:T(8,128)(2,1)}, f32[2,512,512]{2,1,0:T(8,128)}, f32[4096,128]{1,0:T(8,128)}, /*index=5*/f32[8,128]{1,0:T(8,128)}) custom-call(s32[1,80]{1,0:T(1,128)} %bitcast.10, s32[1,80]{1,0:T(1,128)} %bitcast.11, bf16[80,2048]{1,0:T(8,128)(2,1)} %grad.1, ...), custom_call_target="tpu_custom_call" | custom-call | flops 18790481920 | bytes 33554432 | tf_op jit(solution)/shard_map/travel/pallas_call | solution.py:214
  47.2 0.0 copy-start
  47.2 0.0 copy-start.1
  47.2 3.6 %all-to-all-start = ((f32[128,32,128]{2,1,0:T(8,128)}), f32[128,32,128]{2,1,0:T(8,128)S(1)}, u32[]{:S(2)}, u32[]{:S(2)}) async-start(f32[128,32,128]{2,1,0:T(8,128)} %bitcast.9), calls=%async_computation | async-start | bytes 4194304 | tf_op jit(solution)/shard_map/all_to_all | solution.py:392
  50.8 0.0 copy-done
  50.8 0.0 copy-done.1
  50.9 0.1 and_reduce_fusion
  51.0 0.5 convert_element_type.3.live
  51.5 36.1 %refresh.1 = (f32[2,512,512]{2,1,0:T(8,128)}, f32[2,512,512]{2,1,0:T(8,128)}, f32[2,512,512]{2,1,0:T(8,128)}, f32[2,512,512]{2,1,0:T(8,128)}, f32[2,512,512]{2,1,0:T(8,128)}, /*index=5*/f32[2,512,512]{2,1,0:T(8,128)}) custom-call(s32[2]{0:T(128)} %convert_element_type.3.live, f32[8,128]{1,0:T(8,128)} %get-tuple-element.19.clip_ref, ...), custom_call_target="tpu_custom_call" | custom-call | flops 26843545600 | bytes 31457280 | tf_op jit(solution)/shard_map/refresh/pallas_call | solution.py:341
  87.7 0.0 all-to-all-done
  87.7 0.7 gather_fusion
  88.3 1.1 %bitcast_select_fusion = f32[80,2048]{1,0:T(8,128)} fusion(f32[10,8,16,128]{3,2,1,0:T(8,128)S(1)} %bitcast.8, pred[80]{0:T(512)(128)(4,1)S(1)} %get-tuple-element.31), kind=kLoop, calls=%fused_computation.1 | loop fusion | flops 163840 | bytes 1310800 | tf_op jit(solution)/shard_map/jit(_take)/select_n | solution.py:397
  (2 shorter events, 0.0 us)
Async XLA Ops:
  47.2 3.6 %copy-start = (s32[80]{0:T(128)S(1)}, s32[80]{0:T(128)}, u32[]{:S(2)}) copy-start(s32[80]{0:T(128)} %param.10) | copy-start | bytes 964
  47.2 3.6 %copy-start.1 = (s32[80]{0:T(128)S(1)}, s32[80]{0:T(128)}, u32[]{:S(2)}) copy-start(s32[80]{0:T(128)} %param.11) | copy-start | bytes 964
  47.2 40.4 %all-to-all-start = ((f32[128,32,128]{2,1,0:T(8,128)}), f32[128,32,128]{2,1,0:T(8,128)S(1)}, u32[]{:S(2)}, u32[]{:S(2)}) async-start(f32[128,32,128]{2,1,0:T(8,128)} %bitcast.9), calls=%async_computation | async-start | bytes 4194304 | tf_op jit(solution)/shard_map/all_to_all | solution.py:392

commit v2 on v1

--- a/solution.py
+++ b/solution.py
@@ -83,7 +83,7 @@
 
 def travel_kernel(devices, mp, owner, slot, grad, ls_h, lb_h, rs_h, rb_h, m_h, v_h,
                   a_h, p_h, g_h, rot_h, step_h, clip_out,
-                  stage, away, arr, sq, sqs, x_s, st, bs, mo, vs, g_s, ps, gram, rots, steps,
+                  stage, away, arr, sq, sqs, x_s, st, bs, bh, bl, mo, vs, g_s, ps, gram, rots, steps,
                   in_sem, out_sem, send_sem, recv_sem):
     me = lax.axis_index("dp") * mp + lax.axis_index("mp")
     place = lambda d: {"dp": lax.div(d, mp), "mp": lax.rem(d, mp)}
@@ -113,20 +113,23 @@
     sqs[me] = sq[0]
     pl.semaphore_wait(barrier, devices - 1)
 
-    def send(src, dst, n):
-        def one(i, carry):
-            to = lax.rem(me + i, devices)
-            pltpu.make_async_remote_copy(
-                src_ref=src(to), dst_ref=dst, send_sem=send_sem.at[n], recv_sem=recv_sem.at[n],
-                device_id=place(to), device_id_type=pl.DeviceIdType.MESH,
-            ).start()
-            return carry
-
-        lax.fori_loop(1, devices, one, 0)
-
-    send(lambda to: away.at[0, to], arr.at[0, me], 0)
-    send(lambda to: sq.at[0], sqs.at[me], 2)
-    send(lambda to: away.at[1, to], arr.at[1, me], 1)
+    def one(src, dst, n, to):
+        pltpu.make_async_remote_copy(
+            src_ref=src, dst_ref=dst, send_sem=send_sem.at[n], recv_sem=recv_sem.at[n],
+            device_id=place(to), device_id_type=pl.DeviceIdType.MESH,
+        ).start()
+
+    def send_first(i, carry):
+        to = lax.rem(me + i, devices)
+        one(away.at[0, to], arr.at[0, me], 0, to)
+        return carry
+
+    def send_second(i):
+        to = lax.rem(me + i, devices)
+        one(sq.at[0], sqs.at[me], 2, to)
+        one(away.at[1, to], arr.at[1, me], 1, to)
+
+    lax.fori_loop(1, devices, send_first, 0)
     keep = [pltpu.make_async_copy(away.at[s, me], arr.at[s, me], in_sem.at[6 + s]) for s in range(2)]
     for c in keep:
         c.start()
@@ -134,10 +137,29 @@
     for c in loads[:4]:
         c.wait()
     for b in range(4):
-        ps[b] = KEEP * dot3(split(st[b]), split(bs[b]), 1, 0)
+        bh[b], bl[b] = split(bs[b])
+
+    tiles = N // D
+    each = devices // (4 * tiles)
+
+    def tile_of(n):
+        b = lax.div(n, tiles)
+        at = pl.ds(pl.multiple_of(lax.rem(n, tiles) * D, D), D)
+        ps[b, at, :] = KEEP * dot3(split(st[b, at, :]), (bh[b], bl[b]), 1, 0)
+
+    def send_and_tile(n, carry):
+        for u in range(each):
+            send_second(each * n + each + u)
+        tile_of(n)
+        return carry
+
+    for i in range(1, each):
+        send_second(i)
+    lax.fori_loop(0, 4 * tiles - 1, send_and_tile, 0)
+    ps[3, N - D:, :] = KEEP * dot3(split(st[3, N - D:, :]), (bh[3], bl[3]), 1, 0)
     loads[4].wait()
     for s in range(2):
-        rots[s] = dot3(split(dot3(split(bs[s]), split(mo[s]), 0, 0)), split(bs[2 + s]), 1, 0)
+        rots[s] = dot3(split(dot3((bh[s], bl[s]), split(mo[s]), 0, 0)), (bh[2 + s], bl[2 + s]), 1, 0)
     loads[5].wait()
     most = pl.ds(0, devices - 1)
     outs = []
@@ -172,7 +194,7 @@
             g_s[s, :, c * D:(c + 1) * D] = x_s[c].astype(BF16)
         put(g_s.at[s], g_h.at[s])
         g = g_s[s]
-        l, r = split(bs[s]), split(bs[2 + s])
+        l, r = (bh[s], bl[s]), (bh[2 + s], bl[2 + s])
         t = split(dot2l(l, g, 0, 0))
         rot = clip * dot3(t, r, 1, 0)
         v = KEEP * vs[s] + MIX * rot * rot
@@ -228,6 +250,8 @@
             pltpu.VMEM((4, N, D), F32),
             pltpu.VMEM((4, N, N), F32),
             pltpu.VMEM((4, N, N), F32),
+            pltpu.VMEM((4, N, N), BF16),
+            pltpu.VMEM((4, N, N), BF16),
             pltpu.VMEM((2, N, N), F32),
             pltpu.VMEM((2, N, N), F32),
             pltpu.VMEM((2, N, N), BF16),
@@ -269,7 +293,6 @@
     qs[...] = jnp.zeros_like(qs)
     rs[...] = jnp.zeros_like(rs)
     loads[0].wait()
-    loads[1].wait()
 
     def step(k, carry):
         at = pl.ds(pl.multiple_of(k * D, D), D)
@@ -279,8 +302,13 @@
             here = slice(s * LB, (s + 1) * LB)
             low = slice((s + 1) * LB, D)
             ws = leaf([w_d[b, here, :] for b in range(4)], s, LB)
+            if s == 0:
+                @pl.when(k == 0)
+                def _():
+                    loads[1].wait()
+
             for b in range(4):
-                if b * parts // 4 == s:
+                if b * parts // 4 == s - 1:
                     p_ref[b] = p_ref[b] - dot3((qs[0, b], qs[1, b]), (rs[0, b], rs[1, b]), 1, 0)
             for b in range(4):
                 w_d[b, here, :] = jnp.where(lane < (s + 1) * LB, ws[b], 0.0)

time: 89.7 us -> 92.4 us (1.030)
  starting transfers between devices: 3.59 us -> 6.31 us
    all_to_all x1, starting transfers between devices: 3.59 us -> 6.31 us  [shards(): lax.all_to_all(steps, ('dp', 'mp'), split_axis=0, concat_axis=0, tiled=True)]
  transfers between devices with their start and end apart: 1 -> 1, of which waited for: 0 -> 0; matrix products, arithmetic and copies ran while one was open for 1% -> 1% of each run, Pallas kernels for 40% -> 39%
where the time goes in v2:
time: 92.4 us; the launch traced here: 92.2 us
  Pallas kernels  82.7 us (90%)
  starting transfers between devices  6.31 us (7%)
  other arithmetic  1.74 us (2%)
    pallas_call x1, Pallas kernels, travel(): pl.pallas_call(functools.partial(travel_kernel, devices, mp), out_shape=[...  46.7 us
    pallas_call x1, Pallas kernels, refresh(): pl.pallas_call(refresh_kernel, out_shape=[jax.ShapeDtypeStruct((2, N, N),...  36 us
    all_to_all x1, starting transfers between devices, shards(): lax.all_to_all(steps, ('dp', 'mp'), split_axis=0, concat_axis=0, tiled=True)  6.31 us
  transfers between devices with their start and end apart: 1, of which 0 were waited for; matrix products, arithmetic and copies ran while one was open for 1% of the time, Pallas kernels for 39%

profile of v2, /device:TPU:1, one launch (start us, length us, event | category | flops | bytes accessed | tf_op | source)
XLA Modules:
  0.0 92.2 jit_solution(4519317140499331186)
XLA Ops:
  0.6 46.7 %travel.1 = (f32[4,512,512]{2,1,0:T(8,128)}, f32[4,512,512]{2,1,0:T(8,128)}, bf16[2,512,512]{2,1,0:T(8,128)(2,1)}, f32[2,512,512]{2,1,0:T(8,128)}, f32[4096,128]{1,0:T(8,128)}, /*index=5*/f32[8,128]{1,0:T(8,128)}) custom-call(s32[1,80]{1,0:T(1,128)} %bitcast.10, s32[1,80]{1,0:T(1,128)} %bitcast.11, bf16[80,2048]{1,0:T(8,128)(2,1)} %grad.1, ...), custom_call_target="tpu_custom_call" | custom-call | flops 18790481920 | bytes 33554432 | tf_op jit(solution)/shard_map/travel/pallas_call | solution.py:236
  47.3 0.0 copy-start
  47.3 0.0 copy-start.1
  47.3 6.3 %all-to-all-start = ((f32[128,32,128]{2,1,0:T(8,128)}), f32[128,32,128]{2,1,0:T(8,128)S(1)}, u32[]{:S(2)}, u32[]{:S(2)}) async-start(f32[128,32,128]{2,1,0:T(8,128)} %bitcast.9), calls=%async_computation | async-start | bytes 4194304 | tf_op jit(solution)/shard_map/all_to_all | solution.py:420
  53.7 0.0 copy-done
  53.7 0.0 copy-done.1
  53.7 0.1 and_reduce_fusion
  53.8 0.5 convert_element_type.3.live
  54.3 36.0 %refresh.1 = (f32[2,512,512]{2,1,0:T(8,128)}, f32[2,512,512]{2,1,0:T(8,128)}, f32[2,512,512]{2,1,0:T(8,128)}, f32[2,512,512]{2,1,0:T(8,128)}, f32[2,512,512]{2,1,0:T(8,128)}, /*index=5*/f32[2,512,512]{2,1,0:T(8,128)}) custom-call(s32[2]{0:T(128)} %convert_element_type.3.live, f32[8,128]{1,0:T(8,128)} %get-tuple-element.19.clip_ref, ...), custom_call_target="tpu_custom_call" | custom-call | flops 26843545600 | bytes 31457280 | tf_op jit(solution)/shard_map/refresh/pallas_call | solution.py:369
  90.4 0.0 all-to-all-done
  90.4 0.7 gather_fusion
  91.1 1.1 %bitcast_select_fusion = f32[80,2048]{1,0:T(8,128)} fusion(f32[10,8,16,128]{3,2,1,0:T(8,128)S(1)} %bitcast.8, pred[80]{0:T(512)(128)(4,1)S(1)} %get-tuple-element.31), kind=kLoop, calls=%fused_computation.1 | loop fusion | flops 163840 | bytes 1310800 | tf_op jit(solution)/shard_map/jit(_take)/select_n | solution.py:425
  (2 shorter events, 0.0 us)
Async XLA Ops:
  47.3 6.4 %copy-start = (s32[80]{0:T(128)S(1)}, s32[80]{0:T(128)}, u32[]{:S(2)}) copy-start(s32[80]{0:T(128)} %param.10) | copy-start | bytes 964
  47.3 6.3 %copy-start.1 = (s32[80]{0:T(128)S(1)}, s32[80]{0:T(128)}, u32[]{:S(2)}) copy-start(s32[80]{0:T(128)} %param.11) | copy-start | bytes 964
  47.3 43.1 %all-to-all-start = ((f32[128,32,128]{2,1,0:T(8,128)}), f32[128,32,128]{2,1,0:T(8,128)S(1)}, u32[]{:S(2)}, u32[]{:S(2)}) async-start(f32[128,32,128]{2,1,0:T(8,128)} %bitcast.9), calls=%async_computation | async-start | bytes 4194304 | tf_op jit(solution)/shard_map/all_to_all | solution.py:420
